TPU v7x, 32 devices: a whole 2x2x4 slice. The times are simulated.
32 devices in a mesh: geom: 2 (over x), edge: 4 (over y, core), mode: 4 (over z).
Axes of the slice: x: 2, y: 2, z: 4, core: 2. Of those that a mesh axis runs over, the one named last changes fastest.
Arguments:
- basis: bfloat16 [12288, 1024], P(('geom', 'edge'), 'mode'), parts along dimension 0, may hold values from -6 to 6
- motional: bfloat16 [4, 48, 16, 128, 128], P('geom', 'edge'), parts along dimension 0, may hold values from -0.0017089844 to 0.0017089844
- block_cols: int32 [96, 16], P(('geom', 'edge')), parts along dimension 0, may hold values from 0 to 47, as said below
- block_counts: int32 [96], P(('geom', 'edge')), parts along dimension 0, may hold values from 8 to 16, as said below
Outputs:
- reduced: float32 [4, 1024, 1024], P('geom', 'edge', 'mode'), parts along dimension 0
There are 2 independent parts, one for each index of `geom`. A program takes and returns all parts, laid end to end along the dimension named above; each array names one. Nothing has to cross between parts.
Inputs may be any that keep to these rules, and one draw needn't show every extreme that they name: `block_cols`: block row r's live slots hold distinct block columns within 12 blocks of r (at most r + 12, at least r - 12); slot 0 is r itself; slots at or past block_counts[r] hold r. block_counts[r] never exceeds the number of block columns within 12 blocks of r.
All inputs are finite; a program needn't handle non-finite values.
Results may differ from a plain program's by a relative error of at most 0.0029.
Values may be sent and summed in bfloat16 or wider, within the bound.
A program may use at most 64 MiB of HBM per device.

v0:
```python
import jax
import jax.numpy as jnp
from jax import lax
from jax.sharding import PartitionSpec as P


def padded(x, sides, width):
    for axis, dim in sides:
        size, length = (lax.axis_size(axis), x.shape[dim])
        up = [(i, (i + 1) % size) for i in range(size - 1)]
        down = [(j, i) for i, j in up]
        last = lax.slice_in_dim(x, length - width, length, axis=dim)
        initial = lax.slice_in_dim(x, 0, width, axis=dim)
        before = lax.ppermute(last, axis, up)
        after = lax.ppermute(initial, axis, down)
        x = jnp.concatenate([before, x, after], axis=dim)
    return x


def per_device(basis, motional, block_cols, block_counts):
    rows, cols_local = basis.shape
    nbr, nnz = block_cols.shape
    bsize = motional.shape[-1]
    extended = padded(basis, (("edge", 0),), nbr * bsize)
    tiles = extended.reshape(3 * nbr, bsize, cols_local)
    first_block = lax.axis_index("edge") * nbr
    local_cols = block_cols - first_block + nbr
    live = jnp.arange(nnz, dtype=jnp.int32)[None, :] < block_counts[:, None]
    picked = jnp.take(tiles, local_cols, axis=0)
    picked = jnp.where(live[:, :, None, None], picked, jnp.zeros_like(picked))
    work = jnp.einsum("qbkij,bkjm->qbim", motional, picked, preferred_element_type=jnp.float32)
    work = work.astype(jnp.bfloat16).reshape(2, rows, cols_local)
    partial_sum = jnp.einsum(
        "ri,qrj->qij",
        lax.all_gather(basis, "mode", axis=1, tiled=True),
        work,
        preferred_element_type=jnp.float32,
    )
    total = lax.psum(partial_sum, "edge")
    share = total.shape[1] // lax.axis_size("edge")
    return lax.dynamic_slice_in_dim(total, lax.axis_index("edge") * share, share, 1)


def solution(mesh):
    placed = (
        P(("geom", "edge"), "mode"),
        P("geom", "edge", None, None, None),
        P(("geom", "edge"), None),
        P(("geom", "edge")),
    )
    return jax.shard_map(
        per_device, mesh=mesh, in_specs=placed, out_specs=P("geom", "edge", "mode"), check_vma=False
    )
```

profile of v0, /device:TPU:0, one launch (start us, length us, event | category | flops | bytes accessed | tf_op | source)
XLA Modules:
  0.0 138.8 jit_solution(16012564998397765538)
XLA Ops:
  6.5 0.0 all-gather.2.cloned.1.call-start
  6.5 0.7 all-gather.2.cloned.1.call-update
  7.3 0.0 all-reduce.2.cloned.1.call-start
  7.3 2.4 %collective-permute-start = (bf16[1536,256]{1,0:T(8,128)(2,1)}, bf16[1536,256]{1,0:T(8,128)(2,1)S(1)}, u32[]{:S(2)}, u32[]{:S(2)}) collective-permute-start(bf16[1536,256]{1,0:T(8,128)(2,1)} %param.4), channel_id=1, source_target_pairs={{0,4},{4,8},{8,12},{1,5},{5,9},{9,13},{2,6},{6,10},{10,14},{3,7},{... | collective-permute-start | bytes 2359304 | tf_op jit(solution)/shard_map/ppermute | solution.py:14
  9.7 1.3 collective-permute-start.1
  11.0 0.8 compare_and_fusion
  11.8 0.1 reshape.36
  11.9 0.0 collective-permute-done
  11.9 4.4 %collective-permute-done.1 = bf16[1536,256]{1,0:T(8,128)(2,1)} collective-permute-done((bf16[1536,256]{1,0:T(8,128)(2,1)}, bf16[1536,256]{1,0:T(8,128)(2,1)}, u32[]{:S(2)}, u32[]{:S(2)}) %collective-permute-start.1) | collective-permute-done | bytes 786464 | tf_op jit(solution)/shard_map/ppermute | solution.py:15
  16.3 1.5 %pad_maximum_fusion = bf16[4608,256]{1,0:T(8,128)(2,1)S(1)} fusion(bf16[1536,256]{1,0:T(8,128)(2,1)} %collective-permute-done.1, bf16[1536,256]{1,0:T(8,128)(2,1)} %param.4, bf16[1536,256]{1,0:T(8,128)(2,1)S(1)} %collective-permute-done), kind=kLoop, calls=%fused_computation.13 | loop fusion | flops 7077888 | bytes 4718592 | tf_op jit(solution)/shard_map/concatenate | solution.py:16
  17.9 8.2 %gather_fusion = bf16[192,128,256]{2,1,0:T(8,128)(2,1)} fusion(bf16[36,128,256]{2,1,0:T(8,128)(2,1)S(1)} %bitcast.27, s32[1024]{0:T(1024)S(1)} %pad_clamp_fusion), kind=kCustom, calls=%fused_computation | custom fusion | bytes 25166592 | tf_op jit(solution)/shard_map/jit(_take)/gather | solution.py:29
  26.1 10.5 %fusion.18 = bf16[2,12,128,256]{3,2,0,1:T(8,128)(2,1)S(1)} fusion(bf16[2,12,16,128,128]{4,3,2,1,0:T(8,128)(2,1)} %param.5, bf16[12,16,128,256]{3,2,1,0:T(8,128)(2,1)} %bitcast.28, pred[12,16]{1,0:T(8,128)(4,1)S(1)} %get-tuple-element.5, pred[12,16]{1,0:T(8,128)(4,1)S(1)} %get-tuple-element.7), kind=kOutput, calls=%fused_computation.15 | convolution fusion | flops 3234594816 | bytes 26739072 | tf_op jit(solution)/shard_map/qbkij,bkjm->qbim/dot_general | solution.py:31
  36.6 0.1 copy.8
  36.7 38.4 %all-gather.2.cloned.1.call-done = bf16[1536,1024]{1,0:T(8,128)(2,1)} async-done(((bf16[1536,256]{1,0:T(8,128)(2,1)}), bf16[1536,1024]{1,0:T(8,128)(2,1)}) %all-gather.2.cloned.1.call-update) | async-done | bytes 3145744 | tf_op jit(solution)/shard_map/all_gather | solution.py:35
  75.1 5.0 %fusion.15 = f32[2,1024,256]{1,2,0:T(8,128)} fusion(bf16[2,1536,256]{2,1,0:T(8,128)(2,1)S(1)} %bitcast.29, bf16[1536,1024]{1,0:T(8,128)(2,1)} %all-gather.2.cloned.1.call-done), kind=kOutput, calls=%fused_computation.14 | convolution fusion | flops 1610612736 | bytes 6815744 | tf_op jit(solution)/shard_map/ri,qrj->qij/dot_general | solution.py:33
  80.1 0.0 all-reduce.2.cloned.1.call-update
  80.2 49.7 %all-reduce.2.cloned.1.call-done = f32[2,1024,256]{1,2,0:T(8,128)} async-done(((f32[2,1024,256]{1,2,0:T(8,128)}), f32[2,1024,256]{1,2,0:T(8,128)}) %all-reduce.2.cloned.1.call-update) | async-done | bytes 2097168 | tf_op jit(solution)/shard_map/psum | solution.py:39
  129.9 1.1 constant_dynamic-slice_fusion
  130.9 1.0 copy.10
  (1 shorter events, 0.0 us)
Async XLA Ops:
  6.5 68.5 %all-gather.2.cloned.1.call-start = ((), (), s32[]{:S(2)}) async-start(), calls=%async_computation | async-start | bytes 3932160 | tf_op jit(solution)/shard_map/all_gather | solution.py:35
  7.3 122.6 %all-reduce.2.cloned.1.call-start = ((), (), s32[]{:S(2)}) async-start(), calls=%async_computation.1 | async-start | bytes 4194304 | tf_op jit(solution)/shard_map/psum | solution.py:39
  7.3 4.6 %collective-permute-start = (bf16[1536,256]{1,0:T(8,128)(2,1)}, bf16[1536,256]{1,0:T(8,128)(2,1)S(1)}, u32[]{:S(2)}, u32[]{:S(2)}) collective-permute-start(bf16[1536,256]{1,0:T(8,128)(2,1)} %param.4), channel_id=1, source_target_pairs={{0,4},{4,8},{8,12},{1,5},{5,9},{9,13},{2,6},{6,10},{10,14},{3,7},{... | collective-permute-start | bytes 2359304 | tf_op jit(solution)/shard_map/ppermute | solution.py:14
  9.7 6.6 %collective-permute-start.1 = (bf16[1536,256]{1,0:T(8,128)(2,1)}, bf16[1536,256]{1,0:T(8,128)(2,1)}, u32[]{:S(2)}, u32[]{:S(2)}) collective-permute-start(bf16[1536,256]{1,0:T(8,128)(2,1)} %param.4), channel_id=1, source_target_pairs={{4,0},{8,4},{12,8},{5,1},{9,5},{13,9},{6,2},{10,6},{14,10},{7,3},{... | collective-permute-start | bytes 2359304 | tf_op jit(solution)/shard_map/ppermute | solution.py:15
Sparse Core Ops, SparseCore 0:
  8.9 66.1 all-gather.1
  80.3 49.5 all-reduce.1
where the time goes:
time: 139 us
  waiting for transfers between devices  93.2 us (67%)
  matrix products  15.5 us (11%)
  between operations  13.5 us (10%)
  local copies, waits for them, and re-layouts  10.5 us (8%)
  starting transfers between devices  3.74 us (3%)
  other arithmetic  2.31 us (2%)
    psum x1, waiting for transfers between devices, per_device(): total = lax.psum(partial_sum, 'edge')  49.7 us
    all_gather x1, waiting for transfers between devices, per_device(): lax.all_gather(basis, 'mode', axis=1, tiled=True)  38.4 us
    dot_general x1, matrix products, per_device(): jnp.einsum('qbkij,bkjm->qbim', motional, picked, preferred_element_type=j...  10.5 us
    gather x1, local copies, waits for them, and re-layouts, per_device(): picked = jnp.take(tiles, local_cols, axis=0)  8.21 us
    dot_general x1, matrix products, per_device(): jnp.einsum('ri,qrj->qij', lax.all_gather(basis, 'mode', axis=1, tiled=Tru...  5.05 us
    ppermute x1, waiting for transfers between devices, padded(): after = lax.ppermute(initial, axis, down)  4.43 us
  transfers between devices with their start and end apart: 4, of which 3 were waited for; matrix products, arithmetic and copies ran while one was open for 15% of the time, Pallas kernels for 0%

commit v1 on v0

v1 whole, which is shorter than its diff:
```python
import functools

import jax
import jax.numpy as jnp
from jax import lax
from jax.experimental import pallas as pl
from jax.experimental.pallas import tpu as pltpu
from jax.sharding import PartitionSpec as P

MESH = pl.DeviceIdType.MESH


def kernel(
    n_edge, n_mode,
    cols_ref, counts_ref, basis, motional, out,
    ext, gath, mot, work, mine, to_mate, from_mate, to_chip, from_chip,
    own_sem, mot_sem, halo_send, halo_recv, right_send, right_recv, left_send, left_recv,
    mate_send, mate_recv, chip_send, chip_recv,
):
    edge, mode = lax.axis_index("edge"), lax.axis_index("mode")
    nbr, bs, cl = basis.shape
    nnz = mot.shape[2]
    rows = nbr * bs
    n_chip = n_edge // 2
    share = mine.shape[1]
    per_block = cl // share
    chip, core = lax.div(edge, 2), lax.rem(edge, 2)
    mate = edge + 1 - 2 * core

    barrier = pltpu.get_barrier_semaphore()
    for step in range(1, n_edge):
        pl.semaphore_signal(barrier, inc=1, device_id={"edge": lax.rem(edge + step, n_edge)}, device_id_type=MESH)
    has_left, has_right = mode > 0, mode < n_mode - 1
    has_before, has_after = edge > 0, edge < n_edge - 1

    @pl.when(has_left)
    def _():
        pl.semaphore_signal(barrier, inc=1, device_id={"mode": mode - 1}, device_id_type=MESH)

    @pl.when(has_right)
    def _():
        pl.semaphore_signal(barrier, inc=1, device_id={"mode": mode + 1}, device_id_type=MESH)

    own = [
        pltpu.make_async_copy(basis, ext.at[pl.ds(nbr, nbr)], own_sem.at[0]),
        pltpu.make_async_copy(basis, gath.at[mode], own_sem.at[1]),
    ]

    def mot_copy(r):
        return pltpu.make_async_copy(motional.at[:, r], mot.at[:, r], mot_sem.at[r])

    for copy in own:
        copy.start()
    for r in range(nbr):
        mot_copy(r).start()
    ext[3 * nbr] = jnp.zeros((bs, cl), jnp.bfloat16)

    pl.semaphore_wait(barrier, n_edge - 1 + has_left.astype(jnp.int32) + has_right.astype(jnp.int32))

    def go_right(d):
        block = mode - d
        return pltpu.make_async_remote_copy(
            src_ref=basis if d == 0 else gath.at[block], dst_ref=gath.at[block],
            send_sem=right_send.at[d], recv_sem=right_recv.at[d],
            device_id={"mode": mode + 1}, device_id_type=MESH,
        )

    def go_left(d):
        block = mode + d
        return pltpu.make_async_remote_copy(
            src_ref=basis if d == 0 else gath.at[block], dst_ref=gath.at[block],
            send_sem=left_send.at[d], recv_sem=left_recv.at[d],
            device_id={"mode": mode - 1}, device_id_type=MESH,
        )

    def halo(side):
        return pltpu.make_async_remote_copy(
            src_ref=basis, dst_ref=ext.at[pl.ds(2 * nbr * side, nbr)],
            send_sem=halo_send.at[side], recv_sem=halo_recv.at[side],
            device_id={"edge": edge + 1 - 2 * side}, device_id_type=MESH,
        )

    def landed(dst, sem):
        pltpu.make_async_copy(dst, dst, sem).wait()

    @pl.when(has_after)
    def _():
        halo(0).start()

    @pl.when(has_before)
    def _():
        halo(1).start()

    @pl.when(has_right)
    def _():
        go_right(0).start()

    @pl.when(has_left)
    def _():
        go_left(0).start()

    for copy in own:
        copy.wait()

    @pl.when(has_before)
    def _():
        landed(ext.at[pl.ds(0, nbr)], halo_recv.at[0])

    @pl.when(has_after)
    def _():
        landed(ext.at[pl.ds(2 * nbr, nbr)], halo_recv.at[1])

    first = edge * nbr - nbr

    def block_row(r, carry):
        mot_copy(r).wait()
        count = counts_ref[r]
        tiles = [
            ext[jnp.where(k < count, cols_ref[r, k] - first, 3 * nbr)] for k in range(nnz)
        ]
        rhs = jnp.concatenate(tiles, axis=0)
        at = pl.ds(pl.multiple_of(r * bs, bs), bs)
        for q in range(2):
            lhs = jnp.concatenate([mot[q, r, k] for k in range(nnz)], axis=1)
            product = jnp.dot(lhs, rhs, preferred_element_type=jnp.float32)
            work[at, q * cl:(q + 1) * cl] = product.astype(jnp.bfloat16)
        return carry

    lax.fori_loop(0, nbr, block_row, 0)

    def mate_copy(h):
        return pltpu.make_async_remote_copy(
            src_ref=to_mate.at[h], dst_ref=from_mate.at[h],
            send_sem=mate_send.at[h], recv_sem=mate_recv.at[h],
            device_id={"edge": mate}, device_id_type=MESH,
        )

    def chip_copy(h):
        return pltpu.make_async_remote_copy(
            src_ref=to_chip.at[h], dst_ref=from_chip.at[chip],
            send_sem=chip_send.at[h], recv_sem=chip_recv.at[chip],
            device_id={"edge": 2 * h + core}, device_id_type=MESH,
        )

    def product_of(block):
        left = gath[block].reshape(rows, cl)
        total = lax.dot_general(
            left, work[...], (((0,), (0,)), ((), ())), preferred_element_type=jnp.float32
        )
        for k in range(per_block):
            s = block * per_block + k
            h = lax.div(s, 2)
            part = total[k * share:(k + 1) * share]

            @pl.when(lax.rem(s, 2) != core)
            def _():
                to_mate[h] = part
                mate_copy(h).start()

            @pl.when(lax.rem(s, 2) == core)
            def _():
                mine[h] = part

        for k in range(per_block):
            s = block * per_block + k
            h = lax.div(s, 2)

            @pl.when(lax.rem(s, 2) == core)
            def _():
                landed(from_mate.at[h], mate_recv.at[h])

                @pl.when(h != chip)
                def _():
                    to_chip[h] = mine[h] + from_mate[h]
                    chip_copy(h).start()

    product_of(mode)
    for d in range(1, n_mode):
        @pl.when(mode >= d)
        def _():
            landed(gath.at[mode - d], right_recv.at[d - 1])

            if d < n_mode - 1:
                @pl.when(has_right)
                def _():
                    go_right(d).start()

        @pl.when(mode + d < n_mode)
        def _():
            landed(gath.at[mode + d], left_recv.at[d - 1])

            if d < n_mode - 1:
                @pl.when(has_left)
                def _():
                    go_left(d).start()

        @pl.when(mode >= d)
        def _():
            product_of(mode - d)

        @pl.when(mode + d < n_mode)
        def _():
            product_of(mode + d)

    total = mine[chip] + from_mate[chip]
    for step in range(1, n_chip):
        other = lax.rem(chip + step, n_chip)
        landed(from_chip.at[other], chip_recv.at[other])
        total = total + from_chip[other]
    for q in range(2):
        out[q] = total[:, q * cl:(q + 1) * cl]

    for side, there in ((0, has_after), (1, has_before)):
        @pl.when(there)
        def _():
            halo(side).wait_send()

    for d in range(n_mode - 1):
        @pl.when(has_right & (mode >= d))
        def _():
            go_right(d).wait_send()

        @pl.when(has_left & (mode + d < n_mode))
        def _():
            go_left(d).wait_send()

    for h in range(n_chip):
        mate_copy(h).wait_send()

        @pl.when(h != chip)
        def _():
            chip_copy(h).wait_send()


def per_device(n_edge, n_mode, basis, motional, block_cols, block_counts):
    rows, cl = basis.shape
    nbr, nnz = block_cols.shape
    bs = motional.shape[-1]
    share = cl * n_mode // n_edge
    n_chip = n_edge // 2
    part = (n_chip, share, 2 * cl)
    dma = pltpu.SemaphoreType.DMA
    return pl.pallas_call(
        functools.partial(kernel, n_edge, n_mode),
        out_shape=jax.ShapeDtypeStruct((2, share, cl), jnp.float32),
        in_specs=[
            pl.BlockSpec(memory_space=pltpu.SMEM),
            pl.BlockSpec(memory_space=pltpu.SMEM),
            pl.BlockSpec(memory_space=pl.ANY),
            pl.BlockSpec(memory_space=pl.ANY),
        ],
        out_specs=pl.BlockSpec(memory_space=pltpu.VMEM),
        scratch_shapes=[
            pltpu.VMEM((3 * nbr + 1, bs, cl), jnp.bfloat16),
            pltpu.VMEM((n_mode, nbr, bs, cl), jnp.bfloat16),
            pltpu.VMEM((2, nbr, nnz, bs, bs), jnp.bfloat16),
            pltpu.VMEM((rows, 2 * cl), jnp.bfloat16),
            pltpu.VMEM(part, jnp.float32),
            pltpu.VMEM(part, jnp.float32),
            pltpu.VMEM(part, jnp.float32),
            pltpu.VMEM(part, jnp.float32),
            pltpu.VMEM(part, jnp.float32),
            dma((2,)),
            dma((nbr,)),
            dma((2,)),
            dma((2,)),
            dma((n_mode,)),
            dma((n_mode,)),
            dma((n_mode,)),
            dma((n_mode,)),
            dma((n_chip,)),
            dma((n_chip,)),
            dma((n_chip,)),
            dma((n_chip,)),
        ],
        compiler_params=pltpu.CompilerParams(
            collective_id=0, has_side_effects=True, vmem_limit_bytes=48 * 2**20
        ),
    )(block_cols, block_counts, basis.reshape(nbr, bs, cl), motional)


def solution(mesh):
    placed = (
        P(("geom", "edge"), "mode"),
        P("geom", "edge", None, None, None),
        P(("geom", "edge"), None),
        P(("geom", "edge")),
    )
    return jax.shard_map(
        functools.partial(per_device, mesh.shape["edge"], mesh.shape["mode"]),
        mesh=mesh, in_specs=placed, out_specs=P("geom", "edge", "mode"), check_vma=False,
    )
```

time: 139 us -> 72.5 us (0.52)
  the two profiles are of different devices: /device:TPU:0 before, /device:TPU:1 now
where the time goes in v1:
time: 72.5 us; the launch traced here: 72.3 us
  Pallas kernels  69 us (95%)
  local copies, waits for them, and re-layouts  3.28 us (5%)
    pallas_call x1, Pallas kernels, per_device(): pl.pallas_call(functools.partial(kernel, n_edge, n_mode), out_shape=jax.S...  69 us
    unnamed x7, local copies, waits for them, and re-layouts  3.28 us

profile of v1, /device:TPU:1, one launch (start us, length us, event | category | flops | bytes accessed | tf_op | source)
XLA Modules:
  0.0 72.3 jit_solution(7468562234769937379)
XLA Ops:
  0.0 0.0 copy-start
  0.0 1.1 %copy-done = bf16[1536,256]{1,0:T(8,128)(2,1)S(1)} copy-done((bf16[1536,256]{1,0:T(8,128)(2,1)S(1)}, bf16[1536,256]{1,0:T(8,128)(2,1)}, u32[]{:S(2)}) %copy-start) | copy-done | bytes 786456
  1.1 0.0 copy-start.1
  1.1 0.7 copy-done.1
  1.8 0.0 copy-start.2
  1.8 0.7 copy-done.2
  2.5 69.0 %shard_map.46 = f32[2,256,256]{2,1,0:T(8,128)S(1)} custom-call(s32[12,16]{1,0:T(8,128)S(1)} %copy-done.1, s32[12]{0:T(128)S(1)} %copy-done.2, bf16[12,128,256]{2,1,0:T(8,128)(2,1)S(1)} %bitcast.1, bf16[2,12,16,128,128]{4,3,2,1,0:T(8,128)(2,1)} %motional.1), custom_call_target="tpu_custom_call" | custom-call | tf_op jit(solution)/shard_map/pallas_call | solution.py:243
  71.5 0.8 %copy.6 = f32[2,256,256]{2,1,0:T(8,128)} copy(f32[2,256,256]{2,1,0:T(8,128)S(1)} %shard_map.46) | data formatting | bytes 1048576
Async XLA Ops:
  0.0 1.1 %copy-start = (bf16[1536,256]{1,0:T(8,128)(2,1)S(1)}, bf16[1536,256]{1,0:T(8,128)(2,1)}, u32[]{:S(2)}) copy-start(bf16[1536,256]{1,0:T(8,128)(2,1)} %param.4) | copy-start | bytes 2359300
  1.1 0.7 copy-start.1
  1.8 0.7 copy-start.2

commit v2 on v1

--- a/solution.py
+++ b/solution.py
@@ -13,10 +13,12 @@
 def kernel(
     n_edge, n_mode,
     cols_ref, counts_ref, basis, motional, out,
-    ext, gath, mot, work, mine, to_mate, from_mate, to_chip, from_chip,
+    ext_own, ext_end, gath, mot, work, mine, to_mate, from_mate, to_chip, from_chip,
+    mine_far, to_mate_far, from_mate_far, to_end, from_helper,
     own_sem, mot_sem, halo_send, halo_recv, right_send, right_recv, left_send, left_recv,
-    mate_send, mate_recv, chip_send, chip_recv,
+    mate_send, mate_recv, chip_send, chip_recv, far_send, far_recv, end_recv,
 ):
+    ext = (ext_own, ext_end)
     edge, mode = lax.axis_index("edge"), lax.axis_index("mode")
     nbr, bs, cl = basis.shape
     nnz = mot.shape[2]
@@ -26,6 +28,12 @@
     per_block = cl // share
     chip, core = lax.div(edge, 2), lax.rem(edge, 2)
     mate = edge + 1 - 2 * core
+    is_end = (mode == 0) | (mode == n_mode - 1)
+    is_helper = (mode == 1) | (mode == n_mode - 2)
+    low = (mode < 2).astype(jnp.int32)
+    end = (n_mode - 1) * (1 - low)
+    far = (n_mode - 1) * low
+    helper = end + 2 * low - 1
 
     barrier = pltpu.get_barrier_semaphore()
     for step in range(1, n_edge):
@@ -41,8 +49,19 @@
     def _():
         pl.semaphore_signal(barrier, inc=1, device_id={"mode": mode + 1}, device_id_type=MESH)
 
+    for step in range(1, n_edge):
+        to = lax.rem(edge + step, n_edge)
+
+        @pl.when(is_end)
+        def _():
+            pl.semaphore_signal(barrier, inc=1, device_id={"edge": to, "mode": helper}, device_id_type=MESH)
+
+        @pl.when(is_helper)
+        def _():
+            pl.semaphore_signal(barrier, inc=1, device_id={"edge": to, "mode": end}, device_id_type=MESH)
+
     own = [
-        pltpu.make_async_copy(basis, ext.at[pl.ds(nbr, nbr)], own_sem.at[0]),
+        pltpu.make_async_copy(basis, ext[0].at[pl.ds(nbr, nbr)], own_sem.at[0]),
         pltpu.make_async_copy(basis, gath.at[mode], own_sem.at[1]),
     ]
 
@@ -53,9 +72,11 @@
         copy.start()
     for r in range(nbr):
         mot_copy(r).start()
-    ext[3 * nbr] = jnp.zeros((bs, cl), jnp.bfloat16)
-
-    pl.semaphore_wait(barrier, n_edge - 1 + has_left.astype(jnp.int32) + has_right.astype(jnp.int32))
+    for g in range(2):
+        ext[g][3 * nbr] = jnp.zeros((bs, cl), jnp.bfloat16)
+
+    crossing = (n_edge - 1) * (is_end | is_helper).astype(jnp.int32)
+    pl.semaphore_wait(barrier, n_edge - 1 + has_left.astype(jnp.int32) + has_right.astype(jnp.int32) + crossing)
 
     def go_right(d):
         block = mode - d
@@ -73,10 +94,10 @@
             device_id={"mode": mode - 1}, device_id_type=MESH,
         )
 
-    def halo(side):
-        return pltpu.make_async_remote_copy(
-            src_ref=basis, dst_ref=ext.at[pl.ds(2 * nbr * side, nbr)],
-            send_sem=halo_send.at[side], recv_sem=halo_recv.at[side],
+    def halo(side, g=0):
+        return pltpu.make_async_remote_copy(
+            src_ref=gath.at[end] if g else basis, dst_ref=ext[g].at[pl.ds(2 * nbr * side, nbr)],
+            send_sem=halo_send.at[g, side], recv_sem=halo_recv.at[g, side],
             device_id={"edge": edge + 1 - 2 * side}, device_id_type=MESH,
         )
 
@@ -102,31 +123,34 @@
     for copy in own:
         copy.wait()
 
-    @pl.when(has_before)
-    def _():
-        landed(ext.at[pl.ds(0, nbr)], halo_recv.at[0])
-
-    @pl.when(has_after)
-    def _():
-        landed(ext.at[pl.ds(2 * nbr, nbr)], halo_recv.at[1])
-
+    def halo_landed(g):
+        @pl.when(has_before)
+        def _():
+            landed(ext[g].at[pl.ds(0, nbr)], halo_recv.at[g, 0])
+
+        @pl.when(has_after)
+        def _():
+            landed(ext[g].at[pl.ds(2 * nbr, nbr)], halo_recv.at[g, 1])
+
+    halo_landed(0)
     first = edge * nbr - nbr
 
-    def block_row(r, carry):
-        mot_copy(r).wait()
+    def block_row(g, r, carry):
+        if g == 0:
+            mot_copy(r).wait()
         count = counts_ref[r]
         tiles = [
-            ext[jnp.where(k < count, cols_ref[r, k] - first, 3 * nbr)] for k in range(nnz)
+            ext[g][jnp.where(k < count, cols_ref[r, k] - first, 3 * nbr)] for k in range(nnz)
         ]
         rhs = jnp.concatenate(tiles, axis=0)
         at = pl.ds(pl.multiple_of(r * bs, bs), bs)
         for q in range(2):
             lhs = jnp.concatenate([mot[q, r, k] for k in range(nnz)], axis=1)
             product = jnp.dot(lhs, rhs, preferred_element_type=jnp.float32)
-            work[at, q * cl:(q + 1) * cl] = product.astype(jnp.bfloat16)
+            work[g, at, q * cl:(q + 1) * cl] = product.astype(jnp.bfloat16)
         return carry
 
-    lax.fori_loop(0, nbr, block_row, 0)
+    lax.fori_loop(0, nbr, functools.partial(block_row, 0), 0)
 
     def mate_copy(h):
         return pltpu.make_async_remote_copy(
@@ -142,13 +166,29 @@
             device_id={"edge": 2 * h + core}, device_id_type=MESH,
         )
 
+    def mate_copy_far():
+        return pltpu.make_async_remote_copy(
+            src_ref=to_mate_far, dst_ref=from_mate_far, send_sem=far_send.at[0], recv_sem=far_recv,
+            device_id={"edge": mate}, device_id_type=MESH,
+        )
+
+    def end_copy(s):
+        return pltpu.make_async_remote_copy(
+            src_ref=to_end, dst_ref=from_helper.at[chip], send_sem=far_send.at[1], recv_sem=end_recv.at[chip],
+            device_id={"edge": s, "mode": end}, device_id_type=MESH,
+        )
+
+    def shares_of(block):
+        return [(k, block * per_block + k) for k in range(per_block)]
+
+    def times_work(block, g):
+        return lax.dot_general(
+            gath[block].reshape(rows, cl), work[g], (((0,), (0,)), ((), ())), preferred_element_type=jnp.float32
+        )
+
     def product_of(block):
-        left = gath[block].reshape(rows, cl)
-        total = lax.dot_general(
-            left, work[...], (((0,), (0,)), ((), ())), preferred_element_type=jnp.float32
-        )
-        for k in range(per_block):
-            s = block * per_block + k
+        total = times_work(block, 0)
+        for k, s in shares_of(block):
             h = lax.div(s, 2)
             part = total[k * share:(k + 1) * share]
 
@@ -161,8 +201,7 @@
             def _():
                 mine[h] = part
 
-        for k in range(per_block):
-            s = block * per_block + k
+        for k, s in shares_of(block):
             h = lax.div(s, 2)
 
             @pl.when(lax.rem(s, 2) == core)
@@ -174,13 +213,35 @@
                     to_chip[h] = mine[h] + from_mate[h]
                     chip_copy(h).start()
 
+    def product_for_end():
+        total = times_work(far, 1)
+        for k, s in shares_of(far):
+            part = total[k * share:(k + 1) * share]
+
+            @pl.when(lax.rem(s, 2) != core)
+            def _():
+                to_mate_far[...] = part
+                mate_copy_far().start()
+
+            @pl.when(lax.rem(s, 2) == core)
+            def _():
+                mine_far[...] = part
+
+        for k, s in shares_of(far):
+            @pl.when(lax.rem(s, 2) == core)
+            def _():
+                landed(from_mate_far, far_recv)
+                to_end[...] = mine_far[...] + from_mate_far[...]
+                end_copy(s).start()
+
     product_of(mode)
-    for d in range(1, n_mode):
+    end_own = pltpu.make_async_copy(gath.at[end], ext[1].at[pl.ds(nbr, nbr)], own_sem.at[2])
+    for d in range(1, n_mode - 1):
         @pl.when(mode >= d)
         def _():
             landed(gath.at[mode - d], right_recv.at[d - 1])
 
-            if d < n_mode - 1:
+            if d < n_mode - 2:
                 @pl.when(has_right)
                 def _():
                     go_right(d).start()
@@ -189,11 +250,29 @@
         def _():
             landed(gath.at[mode + d], left_recv.at[d - 1])
 
-            if d < n_mode - 1:
+            if d < n_mode - 2:
                 @pl.when(has_left)
                 def _():
                     go_left(d).start()
 
+        if d == 1:
+            @pl.when(is_helper & has_after)
+            def _():
+                halo(0, 1).start()
+
+            @pl.when(is_helper & has_before)
+            def _():
+                halo(1, 1).start()
+
+            @pl.when(is_helper)
+            def _():
+                end_own.start()
+
+        if d == n_mode - 2:
+            @pl.when(is_helper)
+            def _():
+                product_for_end()
+
         @pl.when(mode >= d)
         def _():
             product_of(mode - d)
@@ -202,20 +281,48 @@
         def _():
             product_of(mode + d)
 
-    total = mine[chip] + from_mate[chip]
-    for step in range(1, n_chip):
-        other = lax.rem(chip + step, n_chip)
-        landed(from_chip.at[other], chip_recv.at[other])
-        total = total + from_chip[other]
-    for q in range(2):
-        out[q] = total[:, q * cl:(q + 1) * cl]
+        if d == 1:
+            @pl.when(is_helper)
+            def _():
+                end_own.wait()
+                halo_landed(1)
+                lax.fori_loop(0, nbr, functools.partial(block_row, 1), 0)
+
+    def reduced_here(s):
+        return jnp.logical_not(is_end & (lax.div(s, per_block) == far))
+
+    def put(total):
+        for q in range(2):
+            out[q] = total[:, q * cl:(q + 1) * cl]
+
+    @pl.when(reduced_here(edge))
+    def _():
+        total = mine[chip] + from_mate[chip]
+        for step in range(1, n_chip):
+            other = lax.rem(chip + step, n_chip)
+            landed(from_chip.at[other], chip_recv.at[other])
+            total = total + from_chip[other]
+        put(total)
+
+    @pl.when(jnp.logical_not(reduced_here(edge)))
+    def _():
+        for other in range(n_chip):
+            landed(from_helper.at[other], end_recv.at[other])
+        total = from_helper[0]
+        for other in range(1, n_chip):
+            total = total + from_helper[other]
+        put(total)
 
     for side, there in ((0, has_after), (1, has_before)):
         @pl.when(there)
         def _():
             halo(side).wait_send()
 
-    for d in range(n_mode - 1):
+        @pl.when(there & is_helper)
+        def _():
+            halo(side, 1).wait_send()
+
+    for d in range(n_mode - 2):
         @pl.when(has_right & (mode >= d))
         def _():
             go_right(d).wait_send()
@@ -225,11 +332,22 @@
             go_left(d).wait_send()
 
     for h in range(n_chip):
-        mate_copy(h).wait_send()
-
-        @pl.when(h != chip)
+        @pl.when(reduced_here(2 * h + 1 - core))
+        def _():
+            mate_copy(h).wait_send()
+
+        @pl.when((h != chip) & reduced_here(2 * h + core))
         def _():
             chip_copy(h).wait_send()
+
+    for k, s in shares_of(far):
+        @pl.when(is_helper & (lax.rem(s, 2) != core))
+        def _():
+            mate_copy_far().wait_send()
+
+        @pl.when(is_helper & (lax.rem(s, 2) == core))
+        def _():
+            end_copy(s).wait_send()
 
 
 def per_device(n_edge, n_mode, basis, motional, block_cols, block_counts):
@@ -252,18 +370,24 @@
         out_specs=pl.BlockSpec(memory_space=pltpu.VMEM),
         scratch_shapes=[
             pltpu.VMEM((3 * nbr + 1, bs, cl), jnp.bfloat16),
+            pltpu.VMEM((3 * nbr + 1, bs, cl), jnp.bfloat16),
             pltpu.VMEM((n_mode, nbr, bs, cl), jnp.bfloat16),
             pltpu.VMEM((2, nbr, nnz, bs, bs), jnp.bfloat16),
-            pltpu.VMEM((rows, 2 * cl), jnp.bfloat16),
-            pltpu.VMEM(part, jnp.float32),
-            pltpu.VMEM(part, jnp.float32),
-            pltpu.VMEM(part, jnp.float32),
-            pltpu.VMEM(part, jnp.float32),
-            pltpu.VMEM(part, jnp.float32),
-            dma((2,)),
+            pltpu.VMEM((2, rows, 2 * cl), jnp.bfloat16),
+            pltpu.VMEM(part, jnp.float32),
+            pltpu.VMEM(part, jnp.float32),
+            pltpu.VMEM(part, jnp.float32),
+            pltpu.VMEM(part, jnp.float32),
+            pltpu.VMEM(part, jnp.float32),
+            pltpu.VMEM(part[1:], jnp.float32),
+            pltpu.VMEM(part[1:], jnp.float32),
+            pltpu.VMEM(part[1:], jnp.float32),
+            pltpu.VMEM(part[1:], jnp.float32),
+            pltpu.VMEM(part, jnp.float32),
+            dma((3,)),
             dma((nbr,)),
-            dma((2,)),
-            dma((2,)),
+            dma((2, 2)),
+            dma((2, 2)),
             dma((n_mode,)),
             dma((n_mode,)),
             dma((n_mode,)),
@@ -271,6 +395,9 @@
             dma((n_chip,)),
             dma((n_chip,)),
             dma((n_chip,)),
+            dma((n_chip,)),
+            dma((2,)),
+            dma(()),
             dma((n_chip,)),
         ],
         compiler_params=pltpu.CompilerParams(

time: 72.5 us -> 60.5 us (0.83)
  the two profiles are of different devices: /device:TPU:1 before, /device:TPU:0 now
where the time goes in v2:
time: 60.5 us; the launch traced here: 60.3 us
  Pallas kernels  57 us (94%)
  local copies, waits for them, and re-layouts  3.28 us (5%)
    pallas_call x1, Pallas kernels, per_device(): pl.pallas_call(functools.partial(kernel, n_edge, n_mode), out_shape=jax.S...  57 us
    unnamed x7, local copies, waits for them, and re-layouts  3.28 us

profile of v2, /device:TPU:0, one launch (start us, length us, event | category | flops | bytes accessed | tf_op | source)
XLA Modules:
  0.0 60.3 jit_solution(7577939629893824640)
XLA Ops:
  0.0 0.0 copy-start
  0.0 1.1 %copy-done = bf16[1536,256]{1,0:T(8,128)(2,1)S(1)} copy-done((bf16[1536,256]{1,0:T(8,128)(2,1)S(1)}, bf16[1536,256]{1,0:T(8,128)(2,1)}, u32[]{:S(2)}) %copy-start) | copy-done | bytes 786456
  1.1 0.0 copy-start.1
  1.1 0.7 %copy-done.1 = s32[12,16]{1,0:T(8,128)S(1)} copy-done((s32[12,16]{1,0:T(8,128)S(1)}, s32[12,16]{1,0:T(8,128)}, u32[]{:S(2)}) %copy-start.1) | copy-done | bytes 792
  1.8 0.0 copy-start.2
  1.8 0.7 %copy-done.2 = s32[12]{0:T(128)S(1)} copy-done((s32[12]{0:T(128)S(1)}, s32[12]{0:T(128)}, u32[]{:S(2)}) %copy-start.2) | copy-done | bytes 72
  2.5 57.0 %shard_map.46 = f32[2,256,256]{2,1,0:T(8,128)S(1)} custom-call(s32[12,16]{1,0:T(8,128)S(1)} %copy-done.1, s32[12]{0:T(128)S(1)} %copy-done.2, bf16[12,128,256]{2,1,0:T(8,128)(2,1)S(1)} %bitcast.1, bf16[2,12,16,128,128]{4,3,2,1,0:T(8,128)(2,1)} %motional.1), custom_call_target="tpu_custom_call" | custom-call | tf_op jit(solution)/shard_map/pallas_call | solution.py:361
  59.5 0.8 %copy.6 = f32[2,256,256]{2,1,0:T(8,128)} copy(f32[2,256,256]{2,1,0:T(8,128)S(1)} %shard_map.46) | data formatting | bytes 1048576
Async XLA Ops:
  0.0 1.1 %copy-start = (bf16[1536,256]{1,0:T(8,128)(2,1)S(1)}, bf16[1536,256]{1,0:T(8,128)(2,1)}, u32[]{:S(2)}) copy-start(bf16[1536,256]{1,0:T(8,128)(2,1)} %param.4) | copy-start | bytes 2359300
  1.1 0.7 %copy-start.1 = (s32[12,16]{1,0:T(8,128)S(1)}, s32[12,16]{1,0:T(8,128)}, u32[]{:S(2)}) copy-start(s32[12,16]{1,0:T(8,128)} %cols_ref.1) | copy-start | bytes 2308
  1.8 0.7 %copy-start.2 = (s32[12]{0:T(128)S(1)}, s32[12]{0:T(128)}, u32[]{:S(2)}) copy-start(s32[12]{0:T(128)} %counts_ref.1) | copy-start | bytes 148

commit v3 on v2

--- a/solution.py
+++ b/solution.py
@@ -210,7 +210,7 @@
 
                 @pl.when(h != chip)
                 def _():
-                    to_chip[h] = mine[h] + from_mate[h]
+                    to_chip[h] = (mine[h] + from_mate[h]).astype(to_chip.dtype)
                     chip_copy(h).start()
 
     def product_for_end():
@@ -231,7 +231,7 @@
             @pl.when(lax.rem(s, 2) == core)
             def _():
                 landed(from_mate_far, far_recv)
-                to_end[...] = mine_far[...] + from_mate_far[...]
+                to_end[...] = (mine_far[...] + from_mate_far[...]).astype(to_end.dtype)
                 end_copy(s).start()
 
     product_of(mode)
@@ -301,16 +301,16 @@
         for step in range(1, n_chip):
             other = lax.rem(chip + step, n_chip)
             landed(from_chip.at[other], chip_recv.at[other])
-            total = total + from_chip[other]
+            total = total + from_chip[other].astype(jnp.float32)
         put(total)
 
     @pl.when(jnp.logical_not(reduced_here(edge)))
     def _():
         for other in range(n_chip):
             landed(from_helper.at[other], end_recv.at[other])
-        total = from_helper[0]
+        total = from_helper[0].astype(jnp.float32)
         for other in range(1, n_chip):
-            total = total + from_helper[other]
+            total = total + from_helper[other].astype(jnp.float32)
         put(total)
 
     for side, there in ((0, has_after), (1, has_before)):
@@ -377,13 +377,13 @@
             pltpu.VMEM(part, jnp.float32),
             pltpu.VMEM(part, jnp.float32),
             pltpu.VMEM(part, jnp.float32),
-            pltpu.VMEM(part, jnp.float32),
-            pltpu.VMEM(part, jnp.float32),
+            pltpu.VMEM(part, jnp.bfloat16),
+            pltpu.VMEM(part, jnp.bfloat16),
             pltpu.VMEM(part[1:], jnp.float32),
             pltpu.VMEM(part[1:], jnp.float32),
             pltpu.VMEM(part[1:], jnp.float32),
-            pltpu.VMEM(part[1:], jnp.float32),
-            pltpu.VMEM(part, jnp.float32),
+            pltpu.VMEM(part[1:], jnp.bfloat16),
+            pltpu.VMEM(part, jnp.bfloat16),
             dma((3,)),
             dma((nbr,)),
             dma((2, 2)),
@@ -401,7 +401,7 @@
             dma((n_chip,)),
         ],
         compiler_params=pltpu.CompilerParams(
-            collective_id=0, has_side_effects=True, vmem_limit_bytes=48 * 2**20
+            collective_id=0, has_side_effects=True, vmem_limit_bytes=60 * 2**20
         ),
     )(block_cols, block_counts, basis.reshape(nbr, bs, cl), motional)
 

time: 60.5 us -> 54.7 us (0.904)
  Pallas kernels: 57 us -> 52.6 us
  local copies, waits for them, and re-layouts: 3.28 us -> 1.87 us
    pallas_call x1, Pallas kernels: 57 us -> 52.6 us  [per_device(): pl.pallas_call(functools.partial(kernel, n_edge, n_mode), out_shape=jax.S...]
    unnamed x7 -> x1, local copies, waits for them, and re-layouts: 3.28 us -> 1.87 us
where the time goes in v3:
time: 54.7 us; the launch traced here: 54.5 us
  Pallas kernels  52.6 us (96%)
  local copies, waits for them, and re-layouts  1.87 us (3%)
    pallas_call x1, Pallas kernels, per_device(): pl.pallas_call(functools.partial(kernel, n_edge, n_mode), out_shape=jax.S...  52.6 us
    unnamed x1, local copies, waits for them, and re-layouts  1.87 us

profile of v3, /device:TPU:0, one launch (start us, length us, event | category | flops | bytes accessed | tf_op | source)
XLA Modules:
  0.0 54.5 jit_solution(646415274538416524)
XLA Ops:
  0.0 52.6 %shard_map.46 = f32[2,256,256]{2,1,0:T(8,128)} custom-call(s32[12,16]{1,0:T(8,128)} %cols_ref.1, s32[12]{0:T(128)} %counts_ref.1, bf16[12,128,256]{2,1,0:T(8,128)(2,1)} %bitcast.1, bf16[2,12,16,128,128]{4,3,2,1,0:T(8,128)(2,1)} %motional.1), custom_call_target="tpu_custom_call" | custom-call | tf_op jit(solution)/shard_map/pallas_call | solution.py:361
  52.6 1.9 %copy.6 = f32[2,256,256]{2,1,0:T(8,128)} copy(f32[2,256,256]{2,1,0:T(8,128)} %shard_map.46) | data formatting | bytes 1048576

commit v4 on v3

--- a/solution.py
+++ b/solution.py
@@ -24,7 +24,7 @@
     nnz = mot.shape[2]
     rows = nbr * bs
     n_chip = n_edge // 2
-    share = mine.shape[1]
+    share = mine.shape[2]
     per_block = cl // share
     chip, core = lax.div(edge, 2), lax.rem(edge, 2)
     mate = edge + 1 - 2 * core
@@ -152,87 +152,94 @@
 
     lax.fori_loop(0, nbr, functools.partial(block_row, 0), 0)
 
-    def mate_copy(h):
-        return pltpu.make_async_remote_copy(
-            src_ref=to_mate.at[h], dst_ref=from_mate.at[h],
-            send_sem=mate_send.at[h], recv_sem=mate_recv.at[h],
+    def mate_copy(h, q):
+        return pltpu.make_async_remote_copy(
+            src_ref=to_mate.at[h, q], dst_ref=from_mate.at[h, q],
+            send_sem=mate_send.at[h, q], recv_sem=mate_recv.at[h, q],
             device_id={"edge": mate}, device_id_type=MESH,
         )
 
-    def chip_copy(h):
-        return pltpu.make_async_remote_copy(
-            src_ref=to_chip.at[h], dst_ref=from_chip.at[chip],
-            send_sem=chip_send.at[h], recv_sem=chip_recv.at[chip],
+    def chip_copy(h, q):
+        return pltpu.make_async_remote_copy(
+            src_ref=to_chip.at[h, q], dst_ref=from_chip.at[chip, q],
+            send_sem=chip_send.at[h, q], recv_sem=chip_recv.at[chip, q],
             device_id={"edge": 2 * h + core}, device_id_type=MESH,
         )
 
-    def mate_copy_far():
-        return pltpu.make_async_remote_copy(
-            src_ref=to_mate_far, dst_ref=from_mate_far, send_sem=far_send.at[0], recv_sem=far_recv,
+    def mate_copy_far(q):
+        return pltpu.make_async_remote_copy(
+            src_ref=to_mate_far.at[q], dst_ref=from_mate_far.at[q],
+            send_sem=far_send.at[0, q], recv_sem=far_recv.at[q],
             device_id={"edge": mate}, device_id_type=MESH,
         )
 
-    def end_copy(s):
-        return pltpu.make_async_remote_copy(
-            src_ref=to_end, dst_ref=from_helper.at[chip], send_sem=far_send.at[1], recv_sem=end_recv.at[chip],
+    def end_copy(s, q):
+        return pltpu.make_async_remote_copy(
+            src_ref=to_end.at[q], dst_ref=from_helper.at[chip, q],
+            send_sem=far_send.at[1, q], recv_sem=end_recv.at[chip, q],
             device_id={"edge": s, "mode": end}, device_id_type=MESH,
         )
 
     def shares_of(block):
         return [(k, block * per_block + k) for k in range(per_block)]
 
-    def times_work(block, g):
+    def times_work(block, g, q):
         return lax.dot_general(
-            gath[block].reshape(rows, cl), work[g], (((0,), (0,)), ((), ())), preferred_element_type=jnp.float32
+            gath[block].reshape(rows, cl), work[g, :, q * cl:(q + 1) * cl], (((0,), (0,)), ((), ())),
+            preferred_element_type=jnp.float32,
         )
 
     def product_of(block):
-        total = times_work(block, 0)
+        for q in range(2):
+            total = times_work(block, 0, q)
+            for k, s in shares_of(block):
+                h = lax.div(s, 2)
+                part = total[k * share:(k + 1) * share]
+
+                @pl.when(lax.rem(s, 2) != core)
+                def _():
+                    to_mate[h, q] = part
+                    mate_copy(h, q).start()
+
+                @pl.when(lax.rem(s, 2) == core)
+                def _():
+                    mine[h, q] = part
+
         for k, s in shares_of(block):
             h = lax.div(s, 2)
-            part = total[k * share:(k + 1) * share]
-
-            @pl.when(lax.rem(s, 2) != core)
-            def _():
-                to_mate[h] = part
-                mate_copy(h).start()
 
             @pl.when(lax.rem(s, 2) == core)
             def _():
-                mine[h] = part
-
-        for k, s in shares_of(block):
-            h = lax.div(s, 2)
-
-            @pl.when(lax.rem(s, 2) == core)
-            def _():
-                landed(from_mate.at[h], mate_recv.at[h])
-
-                @pl.when(h != chip)
-                def _():
-                    to_chip[h] = (mine[h] + from_mate[h]).astype(to_chip.dtype)
-                    chip_copy(h).start()
+                for q in range(2):
+                    landed(from_mate.at[h, q], mate_recv.at[h, q])
+
+                    @pl.when(h != chip)
+                    def _():
+                        to_chip[h, q] = (mine[h, q] + from_mate[h, q]).astype(to_chip.dtype)
+                        chip_copy(h, q).start()
 
     def product_for_end():
-        total = times_work(far, 1)
-        for k, s in shares_of(far):
-            part = total[k * share:(k + 1) * share]
-
-            @pl.when(lax.rem(s, 2) != core)
-            def _():
-                to_mate_far[...] = part
-                mate_copy_far().start()
-
-            @pl.when(lax.rem(s, 2) == core)
-            def _():
-                mine_far[...] = part
+        for q in range(2):
+            total = times_work(far, 1, q)
+            for k, s in shares_of(far):
+                part = total[k * share:(k + 1) * share]
+
+                @pl.when(lax.rem(s, 2) != core)
+                def _():
+                    to_mate_far[q] = part
+                    mate_copy_far(q).start()
+
+                @pl.when(lax.rem(s, 2) == core)
+                def _():
+                    mine_far[q] = part
 
         for k, s in shares_of(far):
             @pl.when(lax.rem(s, 2) == core)
             def _():
-                landed(from_mate_far, far_recv)
-                to_end[...] = (mine_far[...] + from_mate_far[...]).astype(to_end.dtype)
-                end_copy(s).start()
+                for q in range(2):
+                    landed(from_mate_far.at[q], far_recv.at[q])
+                    to_end[q] = (mine_far[q] + from_mate_far[q]).astype(to_end.dtype)
+                    end_copy(s, q).start()
 
     product_of(mode)
     end_own = pltpu.make_async_copy(gath.at[end], ext[1].at[pl.ds(nbr, nbr)], own_sem.at[2])
@@ -291,27 +298,24 @@
     def reduced_here(s):
         return jnp.logical_not(is_end & (lax.div(s, per_block) == far))
 
-    def put(total):
+    @pl.when(reduced_here(edge))
+    def _():
         for q in range(2):
-            out[q] = total[:, q * cl:(q + 1) * cl]
-
-    @pl.when(reduced_here(edge))
-    def _():
-        total = mine[chip] + from_mate[chip]
-        for step in range(1, n_chip):
-            other = lax.rem(chip + step, n_chip)
-            landed(from_chip.at[other], chip_recv.at[other])
-            total = total + from_chip[other].astype(jnp.float32)
-        put(total)
+            total = mine[chip, q] + from_mate[chip, q]
+            for step in range(1, n_chip):
+                other = lax.rem(chip + step, n_chip)
+                landed(from_chip.at[other, q], chip_recv.at[other, q])
+                total = total + from_chip[other, q].astype(jnp.float32)
+            out[q] = total
 
     @pl.when(jnp.logical_not(reduced_here(edge)))
     def _():
-        for other in range(n_chip):
-            landed(from_helper.at[other], end_recv.at[other])
-        total = from_helper[0].astype(jnp.float32)
-        for other in range(1, n_chip):
-            total = total + from_helper[other].astype(jnp.float32)
-        put(total)
+        for q in range(2):
+            total = jnp.zeros((share, cl), jnp.float32)
+            for other in range(n_chip):
+                landed(from_helper.at[other, q], end_recv.at[other, q])
+                total = total + from_helper[other, q].astype(jnp.float32)
+            out[q] = total
 
     for side, there in ((0, has_after), (1, has_before)):
         @pl.when(there)
@@ -334,20 +338,24 @@
     for h in range(n_chip):
         @pl.when(reduced_here(2 * h + 1 - core))
         def _():
-            mate_copy(h).wait_send()
+            for q in range(2):
+                mate_copy(h, q).wait_send()
 
         @pl.when((h != chip) & reduced_here(2 * h + core))
         def _():
-            chip_copy(h).wait_send()
+            for q in range(2):
+                chip_copy(h, q).wait_send()
 
     for k, s in shares_of(far):
         @pl.when(is_helper & (lax.rem(s, 2) != core))
         def _():
-            mate_copy_far().wait_send()
+            for q in range(2):
+                mate_copy_far(q).wait_send()
 
         @pl.when(is_helper & (lax.rem(s, 2) == core))
         def _():
-            end_copy(s).wait_send()
+            for q in range(2):
+                end_copy(s, q).wait_send()
 
 
 def per_device(n_edge, n_mode, basis, motional, block_cols, block_counts):
@@ -356,7 +364,7 @@
     bs = motional.shape[-1]
     share = cl * n_mode // n_edge
     n_chip = n_edge // 2
-    part = (n_chip, share, 2 * cl)
+    part = (n_chip, 2, share, cl)
     dma = pltpu.SemaphoreType.DMA
     return pl.pallas_call(
         functools.partial(kernel, n_edge, n_mode),
@@ -392,13 +400,13 @@
             dma((n_mode,)),
             dma((n_mode,)),
             dma((n_mode,)),
-            dma((n_chip,)),
-            dma((n_chip,)),
-            dma((n_chip,)),
-            dma((n_chip,)),
+            dma((n_chip, 2)),
+            dma((n_chip, 2)),
+            dma((n_chip, 2)),
+            dma((n_chip, 2)),
+            dma((2, 2)),
             dma((2,)),
-            dma(()),
-            dma((n_chip,)),
+            dma((n_chip, 2)),
         ],
         compiler_params=pltpu.CompilerParams(
             collective_id=0, has_side_effects=True, vmem_limit_bytes=60 * 2**20

time: 54.7 us -> 54.9 us (level)
  no operation moved by 1% of the time
where the time goes in v4:
time: 54.9 us; the launch traced here: 54.7 us
  Pallas kernels  52.8 us (96%)
  local copies, waits for them, and re-layouts  1.87 us (3%)
    pallas_call x1, Pallas kernels, per_device(): pl.pallas_call(functools.partial(kernel, n_edge, n_mode), out_shape=jax.S...  52.8 us
    unnamed x1, local copies, waits for them, and re-layouts  1.87 us

profile of v4, /device:TPU:0, one launch (start us, length us, event | category | flops | bytes accessed | tf_op | source)
XLA Modules:
  0.0 54.7 jit_solution(10564412230872772171)
XLA Ops:
  0.0 52.8 %shard_map.46 = f32[2,256,256]{2,1,0:T(8,128)} custom-call(s32[12,16]{1,0:T(8,128)} %cols_ref.1, s32[12]{0:T(128)} %counts_ref.1, bf16[12,128,256]{2,1,0:T(8,128)(2,1)} %bitcast.1, bf16[2,12,16,128,128]{4,3,2,1,0:T(8,128)(2,1)} %motional.1), custom_call_target="tpu_custom_call" | custom-call | tf_op jit(solution)/shard_map/pallas_call | solution.py:369
  52.8 1.9 %copy.6 = f32[2,256,256]{2,1,0:T(8,128)} copy(f32[2,256,256]{2,1,0:T(8,128)} %shard_map.46) | data formatting | bytes 1048576

commit v5 on v3

--- a/solution.py
+++ b/solution.py
@@ -78,19 +78,22 @@
     crossing = (n_edge - 1) * (is_end | is_helper).astype(jnp.int32)
     pl.semaphore_wait(barrier, n_edge - 1 + has_left.astype(jnp.int32) + has_right.astype(jnp.int32) + crossing)
 
-    def go_right(d):
+    def half(c):
+        return pl.ds(c * (nbr // 2), nbr // 2)
+
+    def go_right(d, c):
         block = mode - d
         return pltpu.make_async_remote_copy(
-            src_ref=basis if d == 0 else gath.at[block], dst_ref=gath.at[block],
-            send_sem=right_send.at[d], recv_sem=right_recv.at[d],
+            src_ref=basis.at[half(c)] if d == 0 else gath.at[block, half(c)], dst_ref=gath.at[block, half(c)],
+            send_sem=right_send.at[d, c], recv_sem=right_recv.at[d, c],
             device_id={"mode": mode + 1}, device_id_type=MESH,
         )
 
-    def go_left(d):
+    def go_left(d, c):
         block = mode + d
         return pltpu.make_async_remote_copy(
-            src_ref=basis if d == 0 else gath.at[block], dst_ref=gath.at[block],
-            send_sem=left_send.at[d], recv_sem=left_recv.at[d],
+            src_ref=basis.at[half(c)] if d == 0 else gath.at[block, half(c)], dst_ref=gath.at[block, half(c)],
+            send_sem=left_send.at[d, c], recv_sem=left_recv.at[d, c],
             device_id={"mode": mode - 1}, device_id_type=MESH,
         )
 
@@ -112,13 +115,33 @@
     def _():
         halo(1).start()
 
-    @pl.when(has_right)
-    def _():
-        go_right(0).start()
-
-    @pl.when(has_left)
-    def _():
-        go_left(0).start()
+    for c in range(2):
+        @pl.when(has_right)
+        def _():
+            go_right(0, c).start()
+
+        @pl.when(has_left)
+        def _():
+            go_left(0, c).start()
+
+    def pass_on(d, c):
+        @pl.when(mode >= d)
+        def _():
+            landed(gath.at[mode - d, half(c)], right_recv.at[d - 1, c])
+
+            if d < n_mode - 2:
+                @pl.when(has_right)
+                def _():
+                    go_right(d, c).start()
+
+        @pl.when(mode + d < n_mode)
+        def _():
+            landed(gath.at[mode + d, half(c)], left_recv.at[d - 1, c])
+
+            if d < n_mode - 2:
+                @pl.when(has_left)
+                def _():
+                    go_left(d, c).start()
 
     for copy in own:
         copy.wait()
@@ -150,7 +173,10 @@
             work[g, at, q * cl:(q + 1) * cl] = product.astype(jnp.bfloat16)
         return carry
 
-    lax.fori_loop(0, nbr, functools.partial(block_row, 0), 0)
+    lax.fori_loop(0, nbr // 2, functools.partial(block_row, 0), 0)
+    pass_on(1, 0)
+    lax.fori_loop(nbr // 2, nbr, functools.partial(block_row, 0), 0)
+    pass_on(1, 1)
 
     def mate_copy(h):
         return pltpu.make_async_remote_copy(
@@ -234,26 +260,11 @@
                 to_end[...] = (mine_far[...] + from_mate_far[...]).astype(to_end.dtype)
                 end_copy(s).start()
 
-    product_of(mode)
     end_own = pltpu.make_async_copy(gath.at[end], ext[1].at[pl.ds(nbr, nbr)], own_sem.at[2])
     for d in range(1, n_mode - 1):
-        @pl.when(mode >= d)
-        def _():
-            landed(gath.at[mode - d], right_recv.at[d - 1])
-
-            if d < n_mode - 2:
-                @pl.when(has_right)
-                def _():
-                    go_right(d).start()
-
-        @pl.when(mode + d < n_mode)
-        def _():
-            landed(gath.at[mode + d], left_recv.at[d - 1])
-
-            if d < n_mode - 2:
-                @pl.when(has_left)
-                def _():
-                    go_left(d).start()
+        if d > 1:
+            pass_on(d, 0)
+            pass_on(d, 1)
 
         if d == 1:
             @pl.when(is_helper & has_after)
@@ -267,6 +278,8 @@
             @pl.when(is_helper)
             def _():
                 end_own.start()
+
+            product_of(mode)
 
         if d == n_mode - 2:
             @pl.when(is_helper)
@@ -325,11 +338,13 @@
     for d in range(n_mode - 2):
         @pl.when(has_right & (mode >= d))
         def _():
-            go_right(d).wait_send()
+            for c in range(2):
+                go_right(d, c).wait_send()
 
         @pl.when(has_left & (mode + d < n_mode))
         def _():
-            go_left(d).wait_send()
+            for c in range(2):
+                go_left(d, c).wait_send()
 
     for h in range(n_chip):
         @pl.when(reduced_here(2 * h + 1 - core))
@@ -388,10 +403,10 @@
             dma((nbr,)),
             dma((2, 2)),
             dma((2, 2)),
-            dma((n_mode,)),
-            dma((n_mode,)),
-            dma((n_mode,)),
-            dma((n_mode,)),
+            dma((n_mode, 2)),
+            dma((n_mode, 2)),
+            dma((n_mode, 2)),
+            dma((n_mode, 2)),
             dma((n_chip,)),
             dma((n_chip,)),
             dma((n_chip,)),

time: 54.7 us -> 52 us (0.951)
  the two profiles are of different devices: /device:TPU:0 before, /device:TPU:25 now
where the time goes in v5:
time: 52 us; the launch traced here: 51.8 us
  Pallas kernels  49.9 us (96%)
  local copies, waits for them, and re-layouts  1.87 us (4%)
    pallas_call x1, Pallas kernels, per_device(): pl.pallas_call(functools.partial(kernel, n_edge, n_mode), out_shape=jax.S...  49.9 us
    unnamed x1, local copies, waits for them, and re-layouts  1.87 us

profile of v5, /device:TPU:25, one launch (start us, length us, event | category | flops | bytes accessed | tf_op | source)
XLA Modules:
  0.0 51.8 jit_solution(14226017820245402471)
XLA Ops:
  0.0 49.9 %shard_map.46 = f32[2,256,256]{2,1,0:T(8,128)} custom-call(s32[12,16]{1,0:T(8,128)} %cols_ref.1, s32[12]{0:T(128)} %counts_ref.1, bf16[12,128,256]{2,1,0:T(8,128)(2,1)} %bitcast.1, bf16[2,12,16,128,128]{4,3,2,1,0:T(8,128)(2,1)} %motional.1), custom_call_target="tpu_custom_call" | custom-call | tf_op jit(solution)/shard_map/pallas_call | solution.py:376
  49.9 1.9 %copy.6 = f32[2,256,256]{2,1,0:T(8,128)} copy(f32[2,256,256]{2,1,0:T(8,128)} %shard_map.46) | data formatting | bytes 1048576

commit v6 on v5

--- a/solution.py
+++ b/solution.py
@@ -97,10 +97,17 @@
             device_id={"mode": mode - 1}, device_id_type=MESH,
         )
 
-    def halo(side, g=0):
-        return pltpu.make_async_remote_copy(
-            src_ref=gath.at[end] if g else basis, dst_ref=ext[g].at[pl.ds(2 * nbr * side, nbr)],
-            send_sem=halo_send.at[g, side], recv_sem=halo_recv.at[g, side],
+    def halo(side):
+        return pltpu.make_async_remote_copy(
+            src_ref=basis, dst_ref=ext_own.at[pl.ds(2 * nbr * side, nbr)],
+            send_sem=halo_send.at[0, side], recv_sem=halo_recv.at[0, side],
+            device_id={"edge": edge + 1 - 2 * side}, device_id_type=MESH,
+        )
+
+    def halo_end(side, c):
+        return pltpu.make_async_remote_copy(
+            src_ref=gath.at[end, half(c)], dst_ref=ext_end.at[pl.ds(2 * nbr * side + c * (nbr // 2), nbr // 2)],
+            send_sem=halo_send.at[1 + c, side], recv_sem=halo_recv.at[1 + c, side],
             device_id={"edge": edge + 1 - 2 * side}, device_id_type=MESH,
         )
 
@@ -147,13 +154,15 @@
         copy.wait()
 
     def halo_landed(g):
-        @pl.when(has_before)
-        def _():
-            landed(ext[g].at[pl.ds(0, nbr)], halo_recv.at[g, 0])
-
-        @pl.when(has_after)
-        def _():
-            landed(ext[g].at[pl.ds(2 * nbr, nbr)], halo_recv.at[g, 1])
+        size = nbr // 2 if g else nbr
+        for c in range(1 + g):
+            @pl.when(has_before)
+            def _():
+                landed(ext[g].at[pl.ds(c * size, size)], halo_recv.at[g + c, 0])
+
+            @pl.when(has_after)
+            def _():
+                landed(ext[g].at[pl.ds(2 * nbr + c * size, size)], halo_recv.at[g + c, 1])
 
     halo_landed(0)
     first = edge * nbr - nbr
@@ -173,10 +182,21 @@
             work[g, at, q * cl:(q + 1) * cl] = product.astype(jnp.bfloat16)
         return carry
 
+    def widen(c):
+        @pl.when(is_helper & has_after)
+        def _():
+            halo_end(0, c).start()
+
+        @pl.when(is_helper & has_before)
+        def _():
+            halo_end(1, c).start()
+
     lax.fori_loop(0, nbr // 2, functools.partial(block_row, 0), 0)
     pass_on(1, 0)
+    widen(0)
     lax.fori_loop(nbr // 2, nbr, functools.partial(block_row, 0), 0)
     pass_on(1, 1)
+    widen(1)
 
     def mate_copy(h):
         return pltpu.make_async_remote_copy(
@@ -267,14 +287,6 @@
             pass_on(d, 1)
 
         if d == 1:
-            @pl.when(is_helper & has_after)
-            def _():
-                halo(0, 1).start()
-
-            @pl.when(is_helper & has_before)
-            def _():
-                halo(1, 1).start()
-
             @pl.when(is_helper)
             def _():
                 end_own.start()
@@ -333,7 +345,8 @@
 
         @pl.when(there & is_helper)
         def _():
-            halo(side, 1).wait_send()
+            for c in range(2):
+                halo_end(side, c).wait_send()
 
     for d in range(n_mode - 2):
         @pl.when(has_right & (mode >= d))
@@ -401,8 +414,8 @@
             pltpu.VMEM(part, jnp.bfloat16),
             dma((3,)),
             dma((nbr,)),
-            dma((2, 2)),
-            dma((2, 2)),
+            dma((3, 2)),
+            dma((3, 2)),
             dma((n_mode, 2)),
             dma((n_mode, 2)),
             dma((n_mode, 2)),

time: 52 us -> 52.3 us (level)
  the two profiles are of different devices: /device:TPU:25 before, /device:TPU:0 now
where the time goes in v6:
time: 52.3 us; the launch traced here: 52.1 us
  Pallas kernels  50.2 us (96%)
  local copies, waits for them, and re-layouts  1.87 us (4%)
    pallas_call x1, Pallas kernels, per_device(): pl.pallas_call(functools.partial(kernel, n_edge, n_mode), out_shape=jax.S...  50.2 us
    unnamed x1, local copies, waits for them, and re-layouts  1.87 us

profile of v6, /device:TPU:0, one launch (start us, length us, event | category | flops | bytes accessed | tf_op | source)
XLA Modules:
  0.0 52.1 jit_solution(6179302587415778585)
XLA Ops:
  0.0 50.2 %shard_map.46 = f32[2,256,256]{2,1,0:T(8,128)} custom-call(s32[12,16]{1,0:T(8,128)} %cols_ref.1, s32[12]{0:T(128)} %counts_ref.1, bf16[12,128,256]{2,1,0:T(8,128)(2,1)} %bitcast.1, bf16[2,12,16,128,128]{4,3,2,1,0:T(8,128)(2,1)} %motional.1), custom_call_target="tpu_custom_call" | custom-call | tf_op jit(solution)/shard_map/pallas_call | solution.py:389
  50.2 1.9 %copy.6 = f32[2,256,256]{2,1,0:T(8,128)} copy(f32[2,256,256]{2,1,0:T(8,128)} %shard_map.46) | data formatting | bytes 1048576
